TPU v7x, 32 devices: a whole 2x2x4 slice. The times are simulated.
32 devices in a mesh: groups: 2 (over x), cells: 16 (over z, y, core).
Axes of the slice: x: 2, y: 2, z: 4, core: 2. Of those that a mesh axis runs over, the one named last changes fastest.
Arguments:
- snapshots: float32 [2176, 16384], P('cells', 'groups'), parts along dimension 1, may hold values from -6 to 6
- cell_volume: float32 [16384], P(('groups', 'cells')), parts along dimension 0, may hold values from 0.25 to 4
Outputs:
- modes: float32 [2, 128, 16, 16384], P(None, None, None, ('groups', 'cells')), parts along dimension 3
- upper_factor: float32 [4, 16, 16, 128], P('groups'), parts along dimension 0
There are 2 independent parts, one for each index of `groups`. A program takes and returns all parts, laid end to end along the dimension named above; each array names one. Nothing has to cross between parts.
All inputs are finite; a program needn't handle non-finite values.
Results may differ from a plain program's by a relative error of at most 0.000073.
Values sent between devices are 32-bit elements; how exact they have to be, the bound alone decides.
A program may use at most 128 MiB of HBM per device.

v0:
```python
import functools

import jax
import jax.numpy as jnp
import ml_dtypes
import numpy as np
from jax import lax
from jax.experimental import pallas as pl
from jax.experimental.pallas import tpu as pltpu
from jax.sharding import PartitionSpec as P

NFFT = 256
NF = 128
NB = 16
HALF = NFFT // 2
F8 = 8
GROUPS = NF // F8
BF16 = jnp.bfloat16
F32 = jnp.float32


def window_table():
    steps = np.arange(NFFT)
    freqs = np.arange(NF)
    window = 0.5 - 0.5 * np.cos(2.0 * np.pi * steps / NFFT)
    scale = 1.0 / np.sqrt(NB * np.sum(window * window))
    angle = 2.0 * np.pi * (freqs[:, None] * steps[None, :] % NFFT) / NFFT
    cosine = window[None, :] * np.cos(angle) * scale
    sine = -window[None, :] * np.sin(angle) * scale
    table = np.concatenate([cosine, sine], axis=0).astype(np.float32)
    high = table.astype(ml_dtypes.bfloat16)
    low = (table - high.astype(np.float32)).astype(ml_dtypes.bfloat16)
    return high, low


def split(value):
    high = value.astype(BF16)
    return high, (value - high.astype(F32)).astype(BF16)


def dot3(left, right, dims=(((1,), (0,)), ((), ()))):
    dot = functools.partial(lax.dot_general, dimension_numbers=dims, preferred_element_type=F32)
    return dot(left[0], right[0]) + (dot(left[0], right[1]) + dot(left[1], right[0]))


def same_frequency():
    sub = lax.broadcasted_iota(jnp.int32, (F8, NF), 0)
    lane = lax.broadcasted_iota(jnp.int32, (F8, NF), 1)
    return sub == lane % F8


def transform_chunk(first, load, centre, thi_ref, tlo_ref, w_ref, xhi, xlo, spec_ref, gram_ref, cols):
    for i in range(NB + 1):
        rows = slice(i * HALF, (i + 1) * HALF)
        xhi[rows], xlo[rows] = split(load(i) - centre)

    def one_window(b, _):
        rows = pl.ds(pl.multiple_of(b * HALF, HALF), NFFT)
        value = dot3((thi_ref[...], tlo_ref[...]), (xhi[rows], xlo[rows]))
        for ri in range(2):
            spec_ref[:, pl.ds(pl.multiple_of(ri * NF + b * F8, F8), F8), cols] = value[
                ri * NF : (ri + 1) * NF
            ].reshape(GROUPS, F8, -1)
        return 0

    lax.fori_loop(0, NB, one_window, 0, unroll=2)
    keep = same_frequency()[None]

    def one_group(g, _):
        parts = split(spec_ref[g, :, cols] * w_ref[:, cols])
        full = dot3(parts, parts, (((1,), (1,)), ((), ())))
        real = full[:NF, :NF] + full[NF:, NF:]
        imag = full[:NF, NF:] - full[NF:, :NF]
        for ri, value in enumerate((real, imag)):
            value = jnp.where(keep, value.reshape(NB, F8, NF), 0.0).sum(axis=1)
            gram_ref[ri, g] = value if first else gram_ref[ri, g] + value
        return 0

    lax.fori_loop(0, GROUPS, one_group, 0, unroll=2)


def transform_kernel(width, x_ref, w_ref, thi_ref, tlo_ref, spec_ref, gram_ref, xhi, xlo):
    cells = x_ref.shape[1]
    for at in range(0, cells, width):
        cols = slice(at, at + width)
        centre = jnp.mean(x_ref[:, cols], axis=0, keepdims=True)
        transform_chunk(
            at == 0, lambda i: x_ref[i * HALF : (i + 1) * HALF, cols], centre,
            thi_ref, tlo_ref, w_ref, xhi, xlo, spec_ref, gram_ref, cols,
        )


def transform(series, weight):
    slices, cells = series.shape
    width = min(cells, 256)
    vmem = pl.BlockSpec(memory_space=pltpu.VMEM)
    return pl.pallas_call(
        functools.partial(transform_kernel, width),
        out_shape=(
            jax.ShapeDtypeStruct((GROUPS, 2 * NF, cells), F32),
            jax.ShapeDtypeStruct((2, GROUPS, NB, NF), F32),
        ),
        in_specs=[vmem] * 4,
        out_specs=(vmem, vmem),
        scratch_shapes=[pltpu.VMEM((slices, width), BF16)] * 2,
        compiler_params=pltpu.CompilerParams(vmem_limit_bytes=48 * 2**20),
    )(series, weight, *window_table())


def factor(gram_re, gram_im):
    shape = gram_re.shape
    row = lax.broadcasted_iota(jnp.int32, shape, 1)
    lane = lax.broadcasted_iota(jnp.int32, shape, 2)
    block = lane // F8
    flat = (shape[0] * shape[1], shape[2])
    lane2 = lax.broadcasted_iota(jnp.int32, flat, 1)
    a_re, a_im = gram_re, gram_im
    w_re = (row == block).astype(F32)
    w_im = jnp.zeros(shape, F32)
    for j in range(NB):
        index = j * F8 + lane2 % F8

        def spread(value):
            return jnp.take_along_axis(
                value.reshape(flat), index, axis=1, mode="promise_in_bounds"
            ).reshape(shape)

        c_re, c_im = spread(a_re), spread(a_im)
        inverse = 1.0 / jnp.sqrt(c_re[:, j : j + 1])
        l_re = jnp.where(row > j, c_re * inverse, 0.0)
        l_im = jnp.where(row > j, c_im * inverse, 0.0)

        def eliminate(v_re, v_im):
            p_re, p_im = v_re[:, j : j + 1] * inverse, v_im[:, j : j + 1] * inverse
            return (
                jnp.where(row == j, p_re, v_re - (l_re * p_re - l_im * p_im)),
                jnp.where(row == j, p_im, v_im - (l_re * p_im + l_im * p_re)),
            )

        a_re, a_im = eliminate(a_re, a_im)
        w_re, w_im = eliminate(w_re, w_im)
    a_re = jnp.where(block >= row, a_re, 0.0)
    a_im = jnp.where(block > row, a_im, 0.0)
    return a_re, a_im, w_re, w_im


def modes_kernel(gram_ref, spec_ref, modes_ref, upper_ref, inv):
    @pl.when(pl.program_id(0) == 0)
    def _():
        upper_ref[0], upper_ref[1], inv[0], inv[1] = factor(gram_ref[0], gram_ref[1])

    g = pl.program_id(0)
    sub = lax.broadcasted_iota(jnp.int32, (F8, NB, NF), 0)
    lane = lax.broadcasted_iota(jnp.int32, (F8, NB, NF), 2)
    keep = sub == lane % F8
    real, imag = [
        jnp.where(keep, jnp.broadcast_to(inv[ri, g][None], keep.shape), 0.0).reshape(NF, NF)
        for ri in range(2)
    ]
    matrix = jnp.concatenate(
        [jnp.concatenate([real, imag], axis=1), jnp.concatenate([-imag, real], axis=1)], axis=0
    )
    value = dot3(split(matrix), split(spec_ref[0]))
    modes_ref[...] = value.reshape(2, F8, NB, -1)


def finish(gram, spec):
    cells = spec.shape[2]
    whole = (2, GROUPS, NB, NF)
    return pl.pallas_call(
        modes_kernel,
        grid=(GROUPS,),
        out_shape=(
            jax.ShapeDtypeStruct((2, NF, NB, cells), F32),
            jax.ShapeDtypeStruct(whole, F32),
        ),
        in_specs=[
            pl.BlockSpec(whole, lambda g: (0, 0, 0, 0)),
            pl.BlockSpec((1, 2 * NF, cells), lambda g: (g, 0, 0)),
        ],
        out_specs=(
            pl.BlockSpec((2, F8, NB, cells), lambda g: (0, g, 0, 0)),
            pl.BlockSpec(whole, lambda g: (0, 0, 0, 0)),
        ),
        scratch_shapes=[pltpu.VMEM(whole, F32)],
        compiler_params=pltpu.CompilerParams(vmem_limit_bytes=32 * 2**20),
    )(gram, spec)


def on_device(snapshots, cell_volume):
    cells = cell_volume.shape[0]
    slices = snapshots.shape[0]
    members = lax.axis_size("cells")
    weight = jnp.sqrt(cell_volume / (cells * members))[None]
    blocks = snapshots.reshape(slices, members, cells)
    series = lax.all_to_all(blocks, "cells", split_axis=1, concat_axis=0, tiled=True)[:, 0, :]
    spec, gram = transform(series, weight)
    gram = lax.psum(gram, "cells")
    modes, upper = finish(gram, spec)
    upper = upper.reshape(2, GROUPS, NB, NB, F8).transpose(0, 2, 3, 1, 4).reshape(2, NB, NB, NF)
    return modes, upper


def solution(mesh):
    return jax.shard_map(
        on_device,
        mesh=mesh,
        in_specs=(P("cells", "groups"), P(("groups", "cells"))),
        out_specs=(P(None, None, None, ("groups", "cells")), P("groups", None, None, None)),
        check_vma=False,
    )
```

profile of v0, /device:TPU:25, one launch (start us, length us, event | category | flops | bytes accessed | tf_op | source)
XLA Modules:
  0.0 254.0 jit_solution(10152951779165486139)
XLA Ops:
  7.2 4.9 %copy.14 = f32[17,16,8,512]{3,2,0,1:T(8,128)} copy(f32[17,16,8,512]{3,2,1,0:T(8,128)} %bitcast.18) | data formatting | bytes 8912896 | tf_op jit(solution)/shard_map/reshape | solution.py:195
  12.0 0.0 copy-start.4
  12.0 0.0 copy-start.2
  12.0 0.0 copy-start.3
  12.0 6.5 %all-to-all-start = ((f32[136,16,512]{2,0,1:T(8,128)}), f32[136,16,512]{2,0,1:T(8,128)}, u32[]{:S(2)}, u32[]{:S(2)}) async-start(f32[136,16,512]{2,0,1:T(8,128)} %bitcast.15), calls=%async_computation | async-start | bytes 8912896 | tf_op jit(solution)/shard_map/all_to_all | solution.py:196
  18.6 0.0 all-reduce.2.cloned.1.call-start
  18.6 0.0 copy-done.4
  18.6 91.6 %all-to-all-done = f32[136,16,512]{2,0,1:T(8,128)} async-done(((f32[136,16,512]{2,0,1:T(8,128)}), f32[136,16,512]{2,0,1:T(8,128)}, u32[]{:S(2)}, u32[]{:S(2)}) %all-to-all-start) | async-done | bytes 4456480 | tf_op jit(solution)/shard_map/all_to_all | solution.py:196
  110.2 0.0 copy-done.2
  110.2 0.0 copy-done.3
  110.2 20.2 %shard_map.59 = (f32[16,256,512]{2,1,0:T(8,128)}, f32[2,16,16,128]{3,2,1,0:T(8,128)}) custom-call(f32[2176,512]{1,0:T(8,128)} %bitcast.2.x_ref, f32[1,512]{1,0:T(1,128)S(1)} %bitcast.14, bf16[256,256]{1,0:T(8,128)(2,1)S(1)} %copy-done.3, bf16[256,256]{1,0:T(8,128)(2,1)S(1)} %copy-done.2), custom_call_target="tpu_custom_call" | custom-call | tf_op jit(solution)/shard_map/pallas_call | solution.py:97
  130.4 0.0 all-reduce.2.cloned.1.call-update
  130.5 93.7 %all-reduce.2.cloned.1.call-done.gram_ref = f32[2,16,16,128]{3,2,1,0:T(8,128)} async-done(((f32[2,16,16,128]{3,2,1,0:T(8,128)}), f32[2,16,16,128]{3,2,1,0:T(8,128)}) %all-reduce.2.cloned.1.call-update) | async-done | bytes 262160 | tf_op jit(solution)/shard_map/psum | solution.py:198
  224.2 0.0 copy-start
  224.2 3.4 %copy-done = f32[16,256,512]{2,1,0:T(8,128)S(1)} copy-done((f32[16,256,512]{2,1,0:T(8,128)S(1)}, f32[16,256,512]{2,1,0:T(8,128)}, u32[]{:S(2)}) %copy-start) | copy-done | bytes 8388632
  227.6 0.0 copy-start.1
  227.6 0.9 copy-done.1
  228.5 12.4 %shard_map.60 = (f32[2,128,16,512]{3,2,1,0:T(8,128)}, f32[2,16,16,128]{3,2,1,0:T(8,128)S(1)}) custom-call(f32[2,16,16,128]{3,2,1,0:T(8,128)S(1)} %copy-done.1, f32[16,256,512]{2,1,0:T(8,128)S(1)} %copy-done), custom_call_target="tpu_custom_call" | custom-call | tf_op jit(solution)/shard_map/pallas_call | solution.py:170
  240.9 0.6 copy.9
  241.5 2.8 %copy.10 = f32[2,16,16,16,8]{2,4,3,1,0:T(8,128)} copy(f32[2,16,16,16,8]{1,4,2,3,0:T(8,128)S(1)} %bitcast.16) | data formatting | bytes 524288 | tf_op jit(solution)/shard_map/transpose | solution.py:200
  244.3 2.9 %copy.11 = f32[2,16,16,128]{3,2,1,0:T(8,128)} copy(f32[2,16,16,128]{2,3,1,0:T(8,128)} %bitcast.17) | data formatting | bytes 524288
  (1 shorter events, 0.0 us)
Async XLA Ops:
  12.0 6.6 %copy-start.4 = (f32[512]{0:T(512)S(1)}, f32[512]{0:T(512)}, u32[]{:S(2)}) copy-start(f32[512]{0:T(512)} %param.5) | copy-start | bytes 6148
  12.0 98.2 %copy-start.2 = (bf16[256,256]{1,0:T(8,128)(2,1)S(1)}, bf16[256,256]{1,0:T(8,128)(2,1)}, u32[]{:S(2)}) copy-start(bf16[256,256]{1,0:T(8,128)(2,1)} %constant.8.clone.tlo_ref) | copy-start | bytes 393220
  12.0 98.2 %copy-start.3 = (bf16[256,256]{1,0:T(8,128)(2,1)S(1)}, bf16[256,256]{1,0:T(8,128)(2,1)}, u32[]{:S(2)}) copy-start(bf16[256,256]{1,0:T(8,128)(2,1)} %constant.7.clone.thi_ref) | copy-start | bytes 393220
  12.0 98.1 %all-to-all-start = ((f32[136,16,512]{2,0,1:T(8,128)}), f32[136,16,512]{2,0,1:T(8,128)}, u32[]{:S(2)}, u32[]{:S(2)}) async-start(f32[136,16,512]{2,0,1:T(8,128)} %bitcast.15), calls=%async_computation | async-start | bytes 8912896 | tf_op jit(solution)/shard_map/all_to_all | solution.py:196
  18.6 205.6 %all-reduce.2.cloned.1.call-start = ((), (), s32[]{:S(2)}) async-start(), calls=%async_computation.1 | async-start | bytes 524288 | tf_op jit(solution)/shard_map/psum | solution.py:198
  224.2 3.4 %copy-start = (f32[16,256,512]{2,1,0:T(8,128)S(1)}, f32[16,256,512]{2,1,0:T(8,128)}, u32[]{:S(2)}) copy-start(f32[16,256,512]{2,1,0:T(8,128)} %get-tuple-element.7.spec_ref) | copy-start | bytes 25165828
  227.6 0.9 copy-start.1
Sparse Core Ops, SparseCore 0:
  130.6 93.5 all-reduce.1
where the time goes:
time: 257 us; the launch traced here: 254 us
  waiting for transfers between devices  185 us (72%)
  Pallas kernels  32.6 us (13%)
  local copies, waits for them, and re-layouts  15.4 us (6%)
  between operations  14.1 us (5%)
  starting transfers between devices  6.56 us (3%)
    psum x1, waiting for transfers between devices, on_device(): gram = lax.psum(gram, 'cells')  93.7 us
    all_to_all x1, waiting for transfers between devices, on_device(): lax.all_to_all(blocks, 'cells', split_axis=1, concat_axis=0, tiled=True)  91.6 us
    pallas_call x1, Pallas kernels, transform(): pl.pallas_call(functools.partial(transform_kernel, width), out_shape=(jax...  20.2 us
    pallas_call x1, Pallas kernels, finish(): pl.pallas_call(modes_kernel, grid=(GROUPS,), out_shape=(jax.ShapeDtypeStr...  12.4 us
    unnamed x11, local copies, waits for them, and re-layouts  7.21 us
    all_to_all x1, starting transfers between devices, on_device(): lax.all_to_all(blocks, 'cells', split_axis=1, concat_axis=0, tiled=True)  6.52 us
  transfers between devices with their start and end apart: 2, of which 2 were waited for; matrix products, arithmetic and copies ran while one was open for 0% of the time, Pallas kernels for 0%

commit v1 on v0

--- a/solution.py
+++ b/solution.py
@@ -105,6 +105,84 @@
         scratch_shapes=[pltpu.VMEM((slices, width), BF16)] * 2,
         compiler_params=pltpu.CompilerParams(vmem_limit_bytes=48 * 2**20),
     )(series, weight, *window_table())
+
+
+def peer(members, off):
+    return {"cells": lax.rem(lax.axis_index("cells") + off, members)}
+
+
+def greet(members):
+    barrier = pltpu.get_barrier_semaphore()
+
+    def one(off, _):
+        pl.semaphore_signal(
+            barrier, inc=1, device_id=peer(members, off), device_id_type=pl.DeviceIdType.MESH
+        )
+        return 0
+
+    lax.fori_loop(1, members, one, 0)
+    pl.semaphore_wait(barrier, members - 1)
+
+
+def all_sum(members, part_ref, land, gather, sems):
+    me = lax.axis_index("cells")
+
+    def share(off):
+        return pltpu.make_async_remote_copy(
+            src_ref=part_ref.at[lax.rem(me + off, members)],
+            dst_ref=land.at[off],
+            send_sem=sems.at[0, off],
+            recv_sem=sems.at[1, off],
+            device_id=peer(members, off),
+            device_id_type=pl.DeviceIdType.MESH,
+        )
+
+    def result(off):
+        return pltpu.make_async_remote_copy(
+            src_ref=gather.at[me],
+            dst_ref=gather.at[me],
+            send_sem=sems.at[2, off],
+            recv_sem=sems.at[3, off],
+            device_id=peer(members, off),
+            device_id_type=pl.DeviceIdType.MESH,
+        )
+
+    def loop(body):
+        def one(off, _):
+            body(off)
+            return 0
+
+        lax.fori_loop(1, members, one, 0)
+
+    loop(lambda off: share(off).start())
+    land[0] = part_ref[me]
+    loop(lambda off: share(off).wait())
+    gather[me] = jnp.sum(land[...], axis=0)
+    loop(lambda off: result(off).start())
+    loop(lambda off: result(off).wait())
+
+
+def sum_kernel(members, part_ref, out_ref, land, gather, sems):
+    greet(members)
+    all_sum(members, part_ref, land, gather, sems)
+    out_ref[...] = gather[...]
+
+
+def sum_over_cells(gram, members):
+    parts = gram.reshape(members, -1, NF)
+    vmem = pl.BlockSpec(memory_space=pltpu.VMEM)
+    return pl.pallas_call(
+        functools.partial(sum_kernel, members),
+        out_shape=jax.ShapeDtypeStruct(parts.shape, F32),
+        in_specs=[vmem],
+        out_specs=vmem,
+        scratch_shapes=[
+            pltpu.VMEM(parts.shape, F32),
+            pltpu.VMEM(parts.shape, F32),
+            pltpu.SemaphoreType.DMA((4, members)),
+        ],
+        compiler_params=pltpu.CompilerParams(collective_id=0, has_side_effects=True),
+    )(parts).reshape(gram.shape)
 
 
 def factor(gram_re, gram_im):
@@ -195,7 +273,7 @@
     blocks = snapshots.reshape(slices, members, cells)
     series = lax.all_to_all(blocks, "cells", split_axis=1, concat_axis=0, tiled=True)[:, 0, :]
     spec, gram = transform(series, weight)
-    gram = lax.psum(gram, "cells")
+    gram = sum_over_cells(gram, members)
     modes, upper = finish(gram, spec)
     upper = upper.reshape(2, GROUPS, NB, NB, F8).transpose(0, 2, 3, 1, 4).reshape(2, NB, NB, NF)
     return modes, upper

time: 257 us -> 174 us (0.68)
  waiting for transfers between devices: 185 us -> 91.6 us
  Pallas kernels: 32.6 us -> 58 us
  between operations: 14.1 us -> 0.67 us
    psum x1 -> x0, waiting for transfers between devices: 93.7 us -> none  [on_device(): gram = lax.psum(gram, 'cells')]
    pallas_call x0 -> x1, Pallas kernels: none -> 25.5 us  [sum_over_cells(): pl.pallas_call(functools.partial(sum_kernel, members), out_shape=jax.Shap...]
    unnamed x11 -> x13, local copies, waits for them, and re-layouts: 7.21 us -> 7.91 us
  transfers between devices with their start and end apart: 2 -> 1, of which waited for: 2 -> 1; matrix products, arithmetic and copies ran while one was open for 0% -> 0% of each run, Pallas kernels for 0% -> 0%
where the time goes in v1:
time: 174 us; the launch traced here: 173 us
  waiting for transfers between devices  91.6 us (53%)
  Pallas kernels  58 us (33%)
  local copies, waits for them, and re-layouts  16.1 us (9%)
  starting transfers between devices  6.52 us (4%)
    all_to_all x1, waiting for transfers between devices, on_device(): lax.all_to_all(blocks, 'cells', split_axis=1, concat_axis=0, tiled=True)  91.6 us
    pallas_call x1, Pallas kernels, sum_over_cells(): pl.pallas_call(functools.partial(sum_kernel, members), out_shape=jax.Shap...  25.5 us
    pallas_call x1, Pallas kernels, transform(): pl.pallas_call(functools.partial(transform_kernel, width), out_shape=(jax...  20.2 us
    pallas_call x1, Pallas kernels, finish(): pl.pallas_call(modes_kernel, grid=(GROUPS,), out_shape=(jax.ShapeDtypeStr...  12.4 us
    unnamed x13, local copies, waits for them, and re-layouts  7.91 us
    all_to_all x1, starting transfers between devices, on_device(): lax.all_to_all(blocks, 'cells', split_axis=1, concat_axis=0, tiled=True)  6.52 us
    reshape x1, local copies, waits for them, and re-layouts, on_device(): blocks = snapshots.reshape(slices, members, cells)  4.87 us
  transfers between devices with their start and end apart: 1, of which 1 were waited for; matrix products, arithmetic and copies ran while one was open for 0% of the time, Pallas kernels for 0%

profile of v1, /device:TPU:25, one launch (start us, length us, event | category | flops | bytes accessed | tf_op | source)
XLA Modules:
  0.0 172.9 jit_solution(6264754879073456575)
XLA Ops:
  0.6 4.9 %copy.14 = f32[17,16,8,512]{3,2,0,1:T(8,128)} copy(f32[17,16,8,512]{3,2,1,0:T(8,128)} %bitcast.22) | data formatting | bytes 8912896 | tf_op jit(solution)/shard_map/reshape | solution.py:273
  5.5 0.0 copy-start.5
  5.5 0.0 copy-start.3
  5.5 0.0 copy-start.4
  5.5 6.5 %all-to-all-start = ((f32[136,16,512]{2,0,1:T(8,128)}), f32[136,16,512]{2,0,1:T(8,128)}, u32[]{:S(2)}, u32[]{:S(2)}) async-start(f32[136,16,512]{2,0,1:T(8,128)} %bitcast.19), calls=%async_computation | async-start | bytes 8912896 | tf_op jit(solution)/shard_map/all_to_all | solution.py:274
  12.0 0.0 copy-done.5
  12.0 91.6 %all-to-all-done = f32[136,16,512]{2,0,1:T(8,128)} async-done(((f32[136,16,512]{2,0,1:T(8,128)}), f32[136,16,512]{2,0,1:T(8,128)}, u32[]{:S(2)}, u32[]{:S(2)}) %all-to-all-start) | async-done | bytes 4456480 | tf_op jit(solution)/shard_map/all_to_all | solution.py:274
  103.7 0.0 copy-done.3
  103.7 0.0 copy-done.4
  103.7 20.2 %shard_map.59 = (f32[16,256,512]{2,1,0:T(8,128)}, f32[2,16,16,128]{3,2,1,0:T(8,128)S(1)}) custom-call(f32[2176,512]{1,0:T(8,128)} %bitcast.2.x_ref, f32[1,512]{1,0:T(1,128)S(1)} %bitcast.18, bf16[256,256]{1,0:T(8,128)(2,1)S(1)} %copy-done.4, bf16[256,256]{1,0:T(8,128)(2,1)S(1)} %copy-done.3), custom_call_target="tpu_custom_call" | custom-call | tf_op jit(solution)/shard_map/pallas_call | solution.py:97
  123.8 0.0 copy-start.2
  123.8 0.7 copy-done.2
  124.5 25.5 %shard_map.60 = f32[16,32,128]{2,1,0:T(8,128)} custom-call(f32[16,32,128]{2,1,0:T(8,128)} %bitcast.17), custom_call_target="tpu_custom_call" | custom-call | tf_op jit(solution)/shard_map/pallas_call | solution.py:174
  150.0 0.0 copy-start
  150.0 3.4 %copy-done = f32[16,256,512]{2,1,0:T(8,128)S(1)} copy-done((f32[16,256,512]{2,1,0:T(8,128)S(1)}, f32[16,256,512]{2,1,0:T(8,128)}, u32[]{:S(2)}) %copy-start) | copy-done | bytes 8388632
  153.4 0.0 copy-start.1
  153.4 0.9 copy-done.1
  154.3 12.4 %shard_map.61 = (f32[2,128,16,512]{3,2,1,0:T(8,128)}, f32[2,16,16,128]{3,2,1,0:T(8,128)S(1)}) custom-call(f32[2,16,16,128]{3,2,1,0:T(8,128)S(1)} %bitcast.16, f32[16,256,512]{2,1,0:T(8,128)S(1)} %copy-done), custom_call_target="tpu_custom_call" | custom-call | tf_op jit(solution)/shard_map/pallas_call | solution.py:248
  166.7 0.6 copy.9
  167.3 2.8 %copy.10 = f32[2,16,16,16,8]{2,4,3,1,0:T(8,128)} copy(f32[2,16,16,16,8]{1,4,2,3,0:T(8,128)S(1)} %bitcast.20) | data formatting | bytes 524288 | tf_op jit(solution)/shard_map/transpose | solution.py:278
  170.1 2.9 %copy.11 = f32[2,16,16,128]{3,2,1,0:T(8,128)} copy(f32[2,16,16,128]{2,3,1,0:T(8,128)} %bitcast.21) | data formatting | bytes 524288
  (1 shorter events, 0.0 us)
Async XLA Ops:
  5.5 6.5 %copy-start.5 = (f32[512]{0:T(512)S(1)}, f32[512]{0:T(512)}, u32[]{:S(2)}) copy-start(f32[512]{0:T(512)} %param.5) | copy-start | bytes 6148
  5.5 98.2 %copy-start.3 = (bf16[256,256]{1,0:T(8,128)(2,1)S(1)}, bf16[256,256]{1,0:T(8,128)(2,1)}, u32[]{:S(2)}) copy-start(bf16[256,256]{1,0:T(8,128)(2,1)} %constant.8.clone.tlo_ref) | copy-start | bytes 393220
  5.5 98.2 %copy-start.4 = (bf16[256,256]{1,0:T(8,128)(2,1)S(1)}, bf16[256,256]{1,0:T(8,128)(2,1)}, u32[]{:S(2)}) copy-start(bf16[256,256]{1,0:T(8,128)(2,1)} %constant.7.clone.thi_ref) | copy-start | bytes 393220
  5.5 98.1 %all-to-all-start = ((f32[136,16,512]{2,0,1:T(8,128)}), f32[136,16,512]{2,0,1:T(8,128)}, u32[]{:S(2)}, u32[]{:S(2)}) async-start(f32[136,16,512]{2,0,1:T(8,128)} %bitcast.19), calls=%async_computation | async-start | bytes 8912896 | tf_op jit(solution)/shard_map/all_to_all | solution.py:274
  123.8 0.7 copy-start.2
  150.0 3.4 %copy-start = (f32[16,256,512]{2,1,0:T(8,128)S(1)}, f32[16,256,512]{2,1,0:T(8,128)}, u32[]{:S(2)}) copy-start(f32[16,256,512]{2,1,0:T(8,128)} %get-tuple-element.7.spec_ref) | copy-start | bytes 25165828
  153.4 0.9 copy-start.1

commit v2 on v1

--- a/solution.py
+++ b/solution.py
@@ -15,6 +15,7 @@
 HALF = NFFT // 2
 F8 = 8
 GROUPS = NF // F8
+WIDTH = 256
 BF16 = jnp.bfloat16
 F32 = jnp.float32
 
@@ -73,7 +74,8 @@
         imag = full[:NF, NF:] - full[NF:, :NF]
         for ri, value in enumerate((real, imag)):
             value = jnp.where(keep, value.reshape(NB, F8, NF), 0.0).sum(axis=1)
-            gram_ref[ri, g] = value if first else gram_ref[ri, g] + value
+            rows = pl.ds(pl.multiple_of((ri * GROUPS + g) * NB, NB), NB)
+            gram_ref[rows] = value if first else gram_ref[rows] + value
         return 0
 
     lax.fori_loop(0, GROUPS, one_group, 0, unroll=2)
@@ -98,7 +100,7 @@
         functools.partial(transform_kernel, width),
         out_shape=(
             jax.ShapeDtypeStruct((GROUPS, 2 * NF, cells), F32),
-            jax.ShapeDtypeStruct((2, GROUPS, NB, NF), F32),
+            jax.ShapeDtypeStruct((2 * GROUPS * NB, NF), F32),
         ),
         in_specs=[vmem] * 4,
         out_specs=(vmem, vmem),
@@ -126,10 +128,14 @@
 
 def all_sum(members, part_ref, land, gather, sems):
     me = lax.axis_index("cells")
+    rows = part_ref.shape[0] // members
+
+    def of(member):
+        return pl.ds(pl.multiple_of(member * rows, rows), rows)
 
     def share(off):
         return pltpu.make_async_remote_copy(
-            src_ref=part_ref.at[lax.rem(me + off, members)],
+            src_ref=part_ref.at[of(lax.rem(me + off, members))],
             dst_ref=land.at[off],
             send_sem=sems.at[0, off],
             recv_sem=sems.at[1, off],
@@ -139,8 +145,8 @@
 
     def result(off):
         return pltpu.make_async_remote_copy(
-            src_ref=gather.at[me],
-            dst_ref=gather.at[me],
+            src_ref=gather.at[of(me)],
+            dst_ref=gather.at[of(me)],
             send_sem=sems.at[2, off],
             recv_sem=sems.at[3, off],
             device_id=peer(members, off),
@@ -155,9 +161,9 @@
         lax.fori_loop(1, members, one, 0)
 
     loop(lambda off: share(off).start())
-    land[0] = part_ref[me]
+    land[0] = part_ref[of(me)]
     loop(lambda off: share(off).wait())
-    gather[me] = jnp.sum(land[...], axis=0)
+    gather[of(me)] = jnp.sum(land[...], axis=0)
     loop(lambda off: result(off).start())
     loop(lambda off: result(off).wait())
 
@@ -169,20 +175,118 @@
 
 
 def sum_over_cells(gram, members):
-    parts = gram.reshape(members, -1, NF)
     vmem = pl.BlockSpec(memory_space=pltpu.VMEM)
     return pl.pallas_call(
         functools.partial(sum_kernel, members),
-        out_shape=jax.ShapeDtypeStruct(parts.shape, F32),
+        out_shape=jax.ShapeDtypeStruct(gram.shape, F32),
         in_specs=[vmem],
         out_specs=vmem,
         scratch_shapes=[
-            pltpu.VMEM(parts.shape, F32),
-            pltpu.VMEM(parts.shape, F32),
+            pltpu.VMEM((members, gram.shape[0] // members, NF), F32),
+            pltpu.VMEM(gram.shape, F32),
             pltpu.SemaphoreType.DMA((4, members)),
         ],
         compiler_params=pltpu.CompilerParams(collective_id=0, has_side_effects=True),
-    )(parts).reshape(gram.shape)
+    )(gram)
+
+
+def exchange_kernel(
+    members, width, x_ref, w_ref, thi_ref, tlo_ref, spec_out, gram_out,
+    arrived, spec, xhi, xlo, gram, land, gather, own_sem, send_sem, recv_sem, out_sem, sum_sem,
+):
+    me = lax.axis_index("cells")
+    slices = x_ref.shape[0]
+    cells = x_ref.shape[1] // members
+    chunks = cells // width
+    mine = pl.ds(pl.multiple_of(me * slices, 8), slices)
+
+    def source(member, chunk):
+        return x_ref.at[:, pl.ds(pl.multiple_of(member * cells + chunk * width, width), width)]
+
+    def own(chunk):
+        return pltpu.make_async_copy(
+            source(me, chunk), arrived.at[chunk, mine], own_sem.at[chunk]
+        )
+
+    def remote(chunk, off):
+        return pltpu.make_async_remote_copy(
+            src_ref=source(lax.rem(me + off, members), chunk),
+            dst_ref=arrived.at[chunk, mine],
+            send_sem=send_sem.at[chunk, off],
+            recv_sem=recv_sem.at[chunk, off],
+            device_id=peer(members, off),
+            device_id_type=pl.DeviceIdType.MESH,
+        )
+
+    def store(chunk):
+        cols = slice(chunk * width, (chunk + 1) * width)
+        return pltpu.make_async_copy(
+            spec.at[:, :, cols], spec_out.at[:, :, cols], out_sem.at[chunk]
+        )
+
+    def loop(body):
+        def one(off, _):
+            body(off)
+            return 0
+
+        lax.fori_loop(1, members, one, 0)
+
+    for chunk in range(chunks):
+        own(chunk).start()
+    greet(members)
+    for chunk in range(chunks):
+        for off in sorted(range(1, members), key=lambda off: abs(off - members // 2)):
+            remote(chunk, off).start()
+    for chunk in range(chunks):
+        own(chunk).wait()
+        loop(lambda off: remote(chunk, off).wait_recv())
+        cols = slice(chunk * width, (chunk + 1) * width)
+        centre = jnp.mean(arrived[chunk], axis=0, keepdims=True)
+        transform_chunk(
+            chunk == 0, lambda i: arrived[chunk, i * HALF : (i + 1) * HALF], centre,
+            thi_ref, tlo_ref, w_ref, xhi, xlo, spec, gram, cols,
+        )
+        store(chunk).start()
+    all_sum(members, gram, land, gather, sum_sem)
+    gram_out[...] = gather[...]
+    for chunk in range(chunks):
+        loop(lambda off: remote(chunk, off).wait_send())
+        store(chunk).wait()
+
+
+def exchange(snapshots, weight, members):
+    slices = snapshots.shape[0]
+    cells = weight.shape[1]
+    width = min(cells, WIDTH)
+    chunks = cells // width
+    total = slices * members
+    spec = (GROUPS, 2 * NF, cells)
+    gram = (2 * GROUPS * NB, NF)
+    vmem = pl.BlockSpec(memory_space=pltpu.VMEM)
+    anywhere = pl.BlockSpec(memory_space=pl.ANY)
+    return pl.pallas_call(
+        functools.partial(exchange_kernel, members, width),
+        out_shape=(jax.ShapeDtypeStruct(spec, F32), jax.ShapeDtypeStruct(gram, F32)),
+        in_specs=[anywhere, vmem, vmem, vmem],
+        out_specs=(anywhere, vmem),
+        scratch_shapes=[
+            pltpu.VMEM((chunks, total, width), F32),
+            pltpu.VMEM(spec, F32),
+            pltpu.VMEM((total, width), BF16),
+            pltpu.VMEM((total, width), BF16),
+            pltpu.VMEM(gram, F32),
+            pltpu.VMEM((members, gram[0] // members, NF), F32),
+            pltpu.VMEM(gram, F32),
+            pltpu.SemaphoreType.DMA((chunks,)),
+            pltpu.SemaphoreType.DMA((chunks, members)),
+            pltpu.SemaphoreType.DMA((chunks, members)),
+            pltpu.SemaphoreType.DMA((chunks,)),
+            pltpu.SemaphoreType.DMA((4, members)),
+        ],
+        compiler_params=pltpu.CompilerParams(
+            collective_id=1, has_side_effects=True, vmem_limit_bytes=48 * 2**20
+        ),
+    )(snapshots, weight, *window_table())
 
 
 def factor(gram_re, gram_im):
@@ -222,10 +326,22 @@
     return a_re, a_im, w_re, w_im
 
 
+def by_frequency(upper, out_ref, ri):
+    block = lax.broadcasted_iota(jnp.int32, (NB, NF), 1) // F8
+    turned = [pltpu.roll(upper[g], g * F8, 1) if g else upper[g] for g in range(GROUPS)]
+    for k in range(NB):
+        value = turned[0]
+        for g in range(1, GROUPS):
+            value = jnp.where(block == (g + k) % NB, turned[g], value)
+        out_ref[ri, :, k, :] = pltpu.roll(value, (NF - k * F8) % NF, 1) if k else value
+
+
 def modes_kernel(gram_ref, spec_ref, modes_ref, upper_ref, inv):
     @pl.when(pl.program_id(0) == 0)
     def _():
-        upper_ref[0], upper_ref[1], inv[0], inv[1] = factor(gram_ref[0], gram_ref[1])
+        upper_re, upper_im, inv[0], inv[1] = factor(gram_ref[0], gram_ref[1])
+        for ri, upper in enumerate((upper_re, upper_im)):
+            by_frequency(upper, upper_ref, ri)
 
     g = pl.program_id(0)
     sub = lax.broadcasted_iota(jnp.int32, (F8, NB, NF), 0)
@@ -250,7 +366,7 @@
         grid=(GROUPS,),
         out_shape=(
             jax.ShapeDtypeStruct((2, NF, NB, cells), F32),
-            jax.ShapeDtypeStruct(whole, F32),
+            jax.ShapeDtypeStruct((2, NB, NB, NF), F32),
         ),
         in_specs=[
             pl.BlockSpec(whole, lambda g: (0, 0, 0, 0)),
@@ -258,7 +374,7 @@
         ],
         out_specs=(
             pl.BlockSpec((2, F8, NB, cells), lambda g: (0, g, 0, 0)),
-            pl.BlockSpec(whole, lambda g: (0, 0, 0, 0)),
+            pl.BlockSpec((2, NB, NB, NF), lambda g: (0, 0, 0, 0)),
         ),
         scratch_shapes=[pltpu.VMEM(whole, F32)],
         compiler_params=pltpu.CompilerParams(vmem_limit_bytes=32 * 2**20),
@@ -270,13 +386,14 @@
     slices = snapshots.shape[0]
     members = lax.axis_size("cells")
     weight = jnp.sqrt(cell_volume / (cells * members))[None]
-    blocks = snapshots.reshape(slices, members, cells)
-    series = lax.all_to_all(blocks, "cells", split_axis=1, concat_axis=0, tiled=True)[:, 0, :]
-    spec, gram = transform(series, weight)
-    gram = sum_over_cells(gram, members)
-    modes, upper = finish(gram, spec)
-    upper = upper.reshape(2, GROUPS, NB, NB, F8).transpose(0, 2, 3, 1, 4).reshape(2, NB, NB, NF)
-    return modes, upper
+    if slices % 8 == 0 and cells % WIDTH == 0:
+        spec, gram = exchange(snapshots, weight, members)
+    else:
+        blocks = snapshots.reshape(slices, members, cells)
+        series = lax.all_to_all(blocks, "cells", split_axis=1, concat_axis=0, tiled=True)[:, 0, :]
+        spec, gram = transform(series, weight)
+        gram = sum_over_cells(gram, members)
+    return finish(gram.reshape(2, GROUPS, NB, NF), spec)
 
 
 def solution(mesh):

time: 174 us -> 146 us (0.84)
  waiting for transfers between devices: 91.6 us -> 0 us
  Pallas kernels: 58 us -> 137 us
  local copies, waits for them, and re-layouts: 16.1 us -> 7.45 us
  starting transfers between devices: 6.52 us -> 0 us
    all_to_all x1 -> x0, waiting for transfers between devices: 91.6 us -> none  [on_device(): lax.all_to_all(blocks, 'cells', split_axis=1, concat_axis=0, tiled=True)]
    pallas_call x2 -> x1, Pallas kernels: 45.6 us -> 125 us  [exchange(): pl.pallas_call(functools.partial(exchange_kernel, members, width), out_sh...]
    all_to_all x1 -> x0, starting transfers between devices: 6.52 us -> none  [on_device(): lax.all_to_all(blocks, 'cells', split_axis=1, concat_axis=0, tiled=True)]
    reshape x1 -> x0, local copies, waits for them, and re-layouts: 4.87 us -> none  [on_device(): blocks = snapshots.reshape(slices, members, cells)]
    transpose x1 -> x0, local copies, waits for them, and re-layouts: 2.76 us -> none  [on_device(): upper.reshape(2, GROUPS, NB, NB, F8).transpose(0, 2, 3, 1, 4)]
    unnamed x13 -> x8, local copies, waits for them, and re-layouts: 7.91 us -> 7.45 us
  transfers between devices with their start and end apart: 1 -> 0, of which waited for: 1 -> 0; matrix products, arithmetic and copies ran while one was open for 0% -> 0% of each run, Pallas kernels for 0% -> 0%
where the time goes in v2:
time: 146 us
  Pallas kernels  137 us (94%)
  local copies, waits for them, and re-layouts  7.45 us (5%)
    pallas_call x1, Pallas kernels, exchange(): pl.pallas_call(functools.partial(exchange_kernel, members, width), out_sh...  125 us
    pallas_call x1, Pallas kernels, finish(): pl.pallas_call(modes_kernel, grid=(GROUPS,), out_shape=(jax.ShapeDtypeStr...  12.7 us
    unnamed x8, local copies, waits for them, and re-layouts  7.45 us

profile of v2, /device:TPU:25, one launch (start us, length us, event | category | flops | bytes accessed | tf_op | source)
XLA Modules:
  0.0 146.0 jit_solution(1314206511270036065)
XLA Ops:
  0.6 0.7 multiply_sqrt_fusion
  1.3 0.0 copy-start.1
  1.3 2.3 %copy-done.1 = f32[136,8192]{1,0:T(8,128)S(1)} copy-done((f32[136,8192]{1,0:T(8,128)S(1)}, f32[136,8192]{1,0:T(8,128)}, u32[]{:S(2)}) %copy-start.1) | copy-done | bytes 4456472
  3.6 0.0 copy-start.2
  3.6 0.9 copy-done.2
  4.5 0.0 copy-start.3
  4.5 0.9 copy-done.3
  5.4 124.5 %shard_map.59 = (f32[16,256,512]{2,1,0:T(8,128)}, f32[512,128]{1,0:T(8,128)S(1)}) custom-call(f32[136,8192]{1,0:T(8,128)S(1)} %copy-done.1, f32[1,512]{1,0:T(1,128)S(1)} %bitcast.3, bf16[256,256]{1,0:T(8,128)(2,1)S(1)} %copy-done.3, bf16[256,256]{1,0:T(8,128)(2,1)S(1)} %copy-done.2), custom_call_target="tpu_custom_call" | custom-call | tf_op jit(solution)/shard_map/pallas_call | solution.py:267
  129.9 0.0 copy-start
  129.9 3.4 %copy-done = f32[16,256,512]{2,1,0:T(8,128)S(1)} copy-done((f32[16,256,512]{2,1,0:T(8,128)S(1)}, f32[16,256,512]{2,1,0:T(8,128)}, u32[]{:S(2)}) %copy-start) | copy-done | bytes 8388632
  133.3 12.7 %shard_map.60 = (f32[2,128,16,512]{3,2,1,0:T(8,128)}, f32[2,16,16,128]{3,2,1,0:T(8,128)}) custom-call(f32[2,16,16,128]{3,2,1,0:T(8,128)S(1)} %bitcast.2, f32[16,256,512]{2,1,0:T(8,128)S(1)} %copy-done), custom_call_target="tpu_custom_call" | custom-call | tf_op jit(solution)/shard_map/pallas_call | solution.py:364
Async XLA Ops:
  1.3 2.3 %copy-start.1 = (f32[136,8192]{1,0:T(8,128)S(1)}, f32[136,8192]{1,0:T(8,128)}, u32[]{:S(2)}) copy-start(f32[136,8192]{1,0:T(8,128)} %x_ref.1) | copy-start | bytes 13369348
  3.6 0.9 copy-start.2
  4.5 0.9 copy-start.3
  129.9 3.4 %copy-start = (f32[16,256,512]{2,1,0:T(8,128)S(1)}, f32[16,256,512]{2,1,0:T(8,128)}, u32[]{:S(2)}) copy-start(f32[16,256,512]{2,1,0:T(8,128)} %get-tuple-element.5.spec_ref) | copy-start | bytes 25165828

commit v3 on v2

--- a/solution.py
+++ b/solution.py
@@ -15,7 +15,7 @@
 HALF = NFFT // 2
 F8 = 8
 GROUPS = NF // F8
-WIDTH = 256
+WIDTH = 128
 BF16 = jnp.bfloat16
 F32 = jnp.float32
 
@@ -377,7 +377,7 @@
             pl.BlockSpec((2, NB, NB, NF), lambda g: (0, 0, 0, 0)),
         ),
         scratch_shapes=[pltpu.VMEM(whole, F32)],
-        compiler_params=pltpu.CompilerParams(vmem_limit_bytes=32 * 2**20),
+        compiler_params=pltpu.CompilerParams(vmem_limit_bytes=56 * 2**20),
     )(gram, spec)
 
 

time: 146 us -> 146 us (level)
  local copies, waits for them, and re-layouts: 7.45 us -> 4.79 us
  Pallas kernels: 137 us -> 139 us
    pallas_call x1, Pallas kernels: 12.7 us -> 17.4 us  [finish(): pl.pallas_call(modes_kernel, grid=(GROUPS,), out_shape=(jax.ShapeDtypeStr...]
    pallas_call x1, Pallas kernels: 125 us -> 122 us  [exchange(): pl.pallas_call(functools.partial(exchange_kernel, members, width), out_sh...]
    unnamed x8, local copies, waits for them, and re-layouts: 7.45 us -> 4.79 us
where the time goes in v3:
time: 146 us; the launch traced here: 145 us
  Pallas kernels  139 us (95%)
  local copies, waits for them, and re-layouts  4.79 us (3%)
    pallas_call x1, Pallas kernels, exchange(): pl.pallas_call(functools.partial(exchange_kernel, members, width), out_sh...  122 us
    pallas_call x1, Pallas kernels, finish(): pl.pallas_call(modes_kernel, grid=(GROUPS,), out_shape=(jax.ShapeDtypeStr...  17.4 us
    unnamed x8, local copies, waits for them, and re-layouts  4.79 us

profile of v3, /device:TPU:25, one launch (start us, length us, event | category | flops | bytes accessed | tf_op | source)
XLA Modules:
  0.0 145.2 jit_solution(11631034203228016595)
XLA Ops:
  0.6 0.7 multiply_sqrt_fusion
  1.3 0.0 copy-start
  1.3 2.3 %copy-done = f32[136,8192]{1,0:T(8,128)S(1)} copy-done((f32[136,8192]{1,0:T(8,128)S(1)}, f32[136,8192]{1,0:T(8,128)}, u32[]{:S(2)}) %copy-start) | copy-done | bytes 4456472
  3.6 0.0 copy-start.2
  3.6 0.9 copy-done.2
  4.5 0.0 copy-start.3
  4.5 0.9 copy-done.3
  5.4 121.7 %shard_map.59 = (f32[16,256,512]{2,1,0:T(8,128)}, f32[512,128]{1,0:T(8,128)S(1)}) custom-call(f32[136,8192]{1,0:T(8,128)S(1)} %copy-done, f32[1,512]{1,0:T(1,128)S(1)} %bitcast.3, bf16[256,256]{1,0:T(8,128)(2,1)S(1)} %copy-done.3, bf16[256,256]{1,0:T(8,128)(2,1)S(1)} %copy-done.2), custom_call_target="tpu_custom_call" | custom-call | tf_op jit(solution)/shard_map/pallas_call | solution.py:267
  127.1 0.0 copy-start.1
  127.1 0.7 copy-done.1
  127.8 17.4 %shard_map.60 = (f32[2,128,16,512]{3,2,1,0:T(8,128)}, f32[2,16,16,128]{3,2,1,0:T(8,128)}) custom-call(f32[2,16,16,128]{3,2,1,0:T(8,128)} %bitcast.2, f32[16,256,512]{2,1,0:T(8,128)} %get-tuple-element.5.spec_ref), custom_call_target="tpu_custom_call" | custom-call | tf_op jit(solution)/shard_map/pallas_call | solution.py:364
Async XLA Ops:
  1.3 2.3 %copy-start = (f32[136,8192]{1,0:T(8,128)S(1)}, f32[136,8192]{1,0:T(8,128)}, u32[]{:S(2)}) copy-start(f32[136,8192]{1,0:T(8,128)} %x_ref.1) | copy-start | bytes 13369348
  3.6 0.9 copy-start.2
  4.5 0.9 copy-start.3
  127.1 0.7 copy-start.1

commit v4 on v3

--- a/solution.py
+++ b/solution.py
@@ -377,7 +377,7 @@
             pl.BlockSpec((2, NB, NB, NF), lambda g: (0, 0, 0, 0)),
         ),
         scratch_shapes=[pltpu.VMEM(whole, F32)],
-        compiler_params=pltpu.CompilerParams(vmem_limit_bytes=56 * 2**20),
+        compiler_params=pltpu.CompilerParams(vmem_limit_bytes=32 * 2**20),
     )(gram, spec)
 
 

time: 146 us -> 143 us (0.979)
  Pallas kernels: 139 us -> 134 us
  local copies, waits for them, and re-layouts: 4.79 us -> 7.45 us
    pallas_call x1, Pallas kernels: 17.4 us -> 12.7 us  [finish(): pl.pallas_call(modes_kernel, grid=(GROUPS,), out_shape=(jax.ShapeDtypeStr...]
    unnamed x8, local copies, waits for them, and re-layouts: 4.79 us -> 7.45 us
where the time goes in v4:
time: 143 us
  Pallas kernels  134 us (94%)
  local copies, waits for them, and re-layouts  7.45 us (5%)
    pallas_call x1, Pallas kernels, exchange(): pl.pallas_call(functools.partial(exchange_kernel, members, width), out_sh...  122 us
    pallas_call x1, Pallas kernels, finish(): pl.pallas_call(modes_kernel, grid=(GROUPS,), out_shape=(jax.ShapeDtypeStr...  12.7 us
    unnamed x8, local copies, waits for them, and re-layouts  7.45 us

profile of v4, /device:TPU:25, one launch (start us, length us, event | category | flops | bytes accessed | tf_op | source)
XLA Modules:
  0.0 143.2 jit_solution(6952732086042092838)
XLA Ops:
  0.6 0.7 multiply_sqrt_fusion
  1.3 0.0 copy-start.1
  1.3 2.3 %copy-done.1 = f32[136,8192]{1,0:T(8,128)S(1)} copy-done((f32[136,8192]{1,0:T(8,128)S(1)}, f32[136,8192]{1,0:T(8,128)}, u32[]{:S(2)}) %copy-start.1) | copy-done | bytes 4456472
  3.6 0.0 copy-start.2
  3.6 0.9 copy-done.2
  4.5 0.0 copy-start.3
  4.5 0.9 copy-done.3
  5.4 121.7 %shard_map.59 = (f32[16,256,512]{2,1,0:T(8,128)}, f32[512,128]{1,0:T(8,128)S(1)}) custom-call(f32[136,8192]{1,0:T(8,128)S(1)} %copy-done.1, f32[1,512]{1,0:T(1,128)S(1)} %bitcast.3, bf16[256,256]{1,0:T(8,128)(2,1)S(1)} %copy-done.3, bf16[256,256]{1,0:T(8,128)(2,1)S(1)} %copy-done.2), custom_call_target="tpu_custom_call" | custom-call | tf_op jit(solution)/shard_map/pallas_call | solution.py:267
  127.1 0.0 copy-start
  127.1 3.4 %copy-done = f32[16,256,512]{2,1,0:T(8,128)S(1)} copy-done((f32[16,256,512]{2,1,0:T(8,128)S(1)}, f32[16,256,512]{2,1,0:T(8,128)}, u32[]{:S(2)}) %copy-start) | copy-done | bytes 8388632
  130.5 12.7 %shard_map.60 = (f32[2,128,16,512]{3,2,1,0:T(8,128)}, f32[2,16,16,128]{3,2,1,0:T(8,128)}) custom-call(f32[2,16,16,128]{3,2,1,0:T(8,128)S(1)} %bitcast.2, f32[16,256,512]{2,1,0:T(8,128)S(1)} %copy-done), custom_call_target="tpu_custom_call" | custom-call | tf_op jit(solution)/shard_map/pallas_call | solution.py:364
Async XLA Ops:
  1.3 2.3 %copy-start.1 = (f32[136,8192]{1,0:T(8,128)S(1)}, f32[136,8192]{1,0:T(8,128)}, u32[]{:S(2)}) copy-start(f32[136,8192]{1,0:T(8,128)} %x_ref.1) | copy-start | bytes 13369348
  3.6 0.9 copy-start.2
  4.5 0.9 copy-start.3
  127.1 3.4 %copy-start = (f32[16,256,512]{2,1,0:T(8,128)S(1)}, f32[16,256,512]{2,1,0:T(8,128)}, u32[]{:S(2)}) copy-start(f32[16,256,512]{2,1,0:T(8,128)} %get-tuple-element.5.spec_ref) | copy-start | bytes 25165828
